TPU v7x, 128 devices: a whole 4x4x4 slice. The times are simulated.
128 devices in a mesh: tp: 4 (over z_lo, core), cp: 32 (over y, x, z_hi).
Axes of the slice: x: 4, y: 4, z: 4 (z_hi: 2, z_lo: 2; z = z_hi * 2 + z_lo), core: 2. Of those that a mesh axis runs over, the one named last changes fastest.
Arguments:
- queries: bfloat16 [12288, 32, 128], P('cp', 'tp')
- keys: bfloat16 [12288, 8, 128], P('cp', 'tp')
- values: bfloat16 [12288, 8, 128], P('cp', 'tp'), may hold values from -6 to 6
- positions: int32 [12288], P('cp'), may hold values from 0 to 12287, as said below
Outputs:
- attended: bfloat16 [12288, 32, 128], P('cp', 'tp')
Inputs may be any that keep to these rules, and one draw needn't show every extreme that they name: positions is a permutation of the 12288 positions made of blocks of 192 consecutive ascending positions, each block starting at a multiple of 192 and stored in 192 consecutive rows starting at a multiple of 192; which block lies where is drawn from the seed.
All inputs are finite; a program needn't handle non-finite values.
Results may differ from a plain program's by a relative error of at most 0.0055.
Values may be sent and summed in bfloat16 or wider, within the bound.
A program may use at most 320 MiB of HBM per device.

v0:
```python
import jax
import jax.numpy as jnp
from jax import lax
from jax.sharding import PartitionSpec as P


def key_positions(table, count, span):
    rows = jnp.arange(count, dtype=jnp.int32)
    which = rows // span
    hits = which[:, None] == jnp.arange(table.shape[0], dtype=jnp.int32)[None, :]
    base_offset = jnp.sum(jnp.where(hits, table[None, :], 0), axis=1)
    return base_offset + rows % span


def attend(state, grouped_queries, query_pos, key_rows, value_rows, key_pos, scale):
    peak, total, summed = state
    score = (
        jnp.einsum("qgrd,kgd->grqk", grouped_queries, key_rows, preferred_element_type=jnp.float32)
        * scale
    )
    visible = query_pos[:, None] >= key_pos[None, :]
    score = jnp.where(visible[None, None], score, -jnp.inf)
    fresh = jnp.maximum(peak, jnp.max(score, axis=-1))
    expo = jnp.exp(score - fresh[..., None])
    total = jnp.sum(expo, axis=-1)
    product = jnp.einsum(
        "grqk,kgd->grqd", expo.astype(jnp.bfloat16), value_rows, preferred_element_type=jnp.float32
    )
    summed = product
    return (fresh, total, summed)


def body(queries, keys, values, positions):
    tok = queries.shape[0]
    span = tok // 2
    kv_heads = keys.shape[1]
    heads = queries.shape[1]
    width = queries.shape[2]
    query_group = heads // kv_heads
    scale = width ** (-0.5)
    grouped_queries = queries.reshape(tok, kv_heads, query_group, width)
    starts = jnp.stack([positions[0], positions[span]])
    table = lax.all_gather(starts, "cp", axis=0, tiled=True)
    stacked = jnp.stack([keys, values])
    init = (
        jnp.full((kv_heads, query_group, tok), -1e30, jnp.float32),
        jnp.zeros((kv_heads, query_group, tok), jnp.float32),
        jnp.zeros((kv_heads, query_group, tok, width), jnp.float32),
    )
    piece = lax.all_gather(stacked, "cp", axis=1, tiled=True)
    count = piece.shape[1]
    key_pos = key_positions(table, count, span)
    state = attend(init, grouped_queries, positions, piece[0], piece[1], key_pos, scale)
    peak, total, summed = state
    result = summed / total[..., None]
    return jnp.transpose(result, (2, 0, 1, 3)).reshape(tok, heads, width).astype(jnp.bfloat16)


def solution(mesh):
    return jax.shard_map(
        body,
        mesh=mesh,
        in_specs=(P("cp", "tp", None), P("cp", "tp", None), P("cp", "tp", None), P("cp")),
        out_specs=P("cp", "tp", None),
        check_vma=False,
    )
```

profile of v0, /device:TPU:0, one launch (start us, length us, event | category | flops | bytes accessed | tf_op | source)
XLA Modules:
  0.0 307.5 jit_solution(13351679954990828400)
XLA Ops:
  6.5 0.0 copy-start
  6.5 0.0 all-gather.2.cloned.1.call-start
  6.5 1.1 copy_bitcast_fusion
  7.7 0.8 pad_maximum_fusion
  8.5 0.0 all-gather.2.cloned.1.call-update
  8.5 1.3 dynamic-slice
  10.4 1.4 fusion.21
  11.8 1.4 add_dynamic-update-slice_fusion
  13.2 21.3 %all-reduce = s32[64]{0:T(128)S(1)} all-reduce(s32[64]{0:T(128)S(1)} %add_dynamic-update-slice_fusion), channel_id=1, replica_groups=mesh['tp'=4,'cp'=32] {'cp'}, use_global_device_ids=true, to_apply=%add | all-reduce | flops 64 | bytes 512
  34.5 0.6 select_reduce_fusion
  35.1 7.4 %broadcast_compare_fusion = pred[384,12288]{0,1:T(8,128)(4,1)} fusion(s32[384]{0:T(512)} %param.7, s32[12288]{0:T(1024)S(1)} %fusion.17), kind=kLoop, calls=%fused_computation.7 | loop fusion | flops 4718592 | bytes 4769280 | tf_op jit(solution)/shard_map/ge | solution.py:21
  42.5 100.4 %all-gather.2.cloned.1.call-done = bf16[2,12288,2,128]{3,1,2,0:T(8,128)(2,1)} async-done(((bf16[2,384,2,128]{3,1,2,0:T(8,128)(2,1)}), bf16[2,12288,2,128]{3,1,2,0:T(8,128)(2,1)}) %all-gather.2.cloned.1.call-update) | async-done | bytes 12582928 | tf_op jit(solution)/shard_map/all_gather | solution.py:50
  142.9 0.0 copy-done
  142.9 54.1 %fusion.2 = (f32[2,4,384]{2,1,0:T(4,128)S(1)}, f32[2,12288,384,4]{2,1,3,0:T(8,128)}) fusion(pred[384,12288]{0,1:T(8,128)(4,1)} %broadcast_compare_fusion, bf16[384,2,4,128]{3,2,1,0:T(4,128)(2,1)S(1)} %bitcast.46, bf16[2,12288,2,128]{3,1,2,0:T(8,128)(2,1)} %all-gather.2.cloned.1.call-done), kind=kOutput, calls=%fused_computation.4 | convolution fusion | flops 9776919552 | bytes 162803712 | tf_op jit(solution)/shard_map/qgrd,kgd->grqk/dot_general | solution.py:18
  197.0 47.5 %fusion = f32[2,4,384]{2,1,0:T(4,128)S(1)} fusion(f32[2,12288,384,4]{2,1,3,0:T(8,128)} %get-tuple-element.8, f32[2,4,384]{2,1,0:T(4,128)S(1)} %broadcast_maximum_fusion, pred[384,12288]{0,1:T(8,128)(4,1)} %broadcast_compare_fusion), kind=kLoop, calls=%fused_computation.2 | loop fusion | flops 150991872 | bytes 155738112 | tf_op jit(solution)/shard_map/reduce_sum | solution.py:25
  244.6 54.7 %fusion.7 = bf16[384,2,4,128]{3,0,2,1:T(8,128)(2,1)S(1)} fusion(bf16[2,12288,2,128]{3,1,2,0:T(8,128)(2,1)} %all-gather.2.cloned.1.call-done, f32[2,12288,384,4]{2,1,3,0:T(8,128)} %get-tuple-element.8, f32[2,4,384]{2,1,0:T(4,128)S(1)} %broadcast_maximum_fusion, pred[384,12288]{0,1:T(8,128)(4,1)} %broadcast_compare_fusion, f32[384,2,4]{0,2,1:T(4,128)S(1)} %bitcast.48), kind=kOutput, calls=%fused_computation.14 | convolution fusion | flops 9815457792 | bytes 162816000 | tf_op jit(solution)/shard_map/grqk,kgd->grqd/dot_general | solution.py:26
  299.2 1.4 copy.14
  (4 shorter events, 0.0 us)
Async XLA Ops:
  6.5 136.4 %copy-start = (bf16[384,8,128]{2,1,0:T(8,128)(2,1)S(1)}, bf16[384,8,128]{2,1,0:T(8,128)(2,1)}, u32[]{:S(2)}) copy-start(bf16[384,8,128]{2,1,0:T(8,128)(2,1)} %param.4) | copy-start | bytes 2359300
  6.5 136.4 %all-gather.2.cloned.1.call-start = ((), (), s32[]{:S(2)}) async-start(), calls=%async_computation | async-start | bytes 12976128 | tf_op jit(solution)/shard_map/all_gather | solution.py:50
Sparse Core Ops, SparseCore 0:
  10.3 132.5 all-gather.1
where the time goes:
time: 308 us; the launch traced here: 307 us
  matrix products  109 us (35%)
  waiting for transfers between devices  100 us (32%)
  other arithmetic  57.7 us (19%)
  blocking collectives  21.3 us (7%)
  between operations  14.1 us (5%)
  local copies, waits for them, and re-layouts  5.16 us (2%)
    all_gather x1, waiting for transfers between devices, body(): piece = lax.all_gather(stacked, 'cp', axis=1, tiled=True)  100 us
    dot_general x1, matrix products, attend(): jnp.einsum('grqk,kgd->grqd', expo.astype(jnp.bfloat16), value_rows, prefe...  54.7 us
    dot_general x1, matrix products, attend(): jnp.einsum('qgrd,kgd->grqk', grouped_queries, key_rows, preferred_element...  54.1 us
    reduce_sum x1, other arithmetic, attend(): total = jnp.sum(expo, axis=-1)  47.5 us
    unnamed x1, blocking collectives  21.3 us
    ge x1, other arithmetic, attend(): visible = query_pos[:, None] >= key_pos[None, :]  7.42 us
  transfers between devices with their start and end apart: 1, of which 1 were waited for; matrix products, arithmetic and copies ran while one was open for 4% of the time, Pallas kernels for 0%

commit v1 on v0

v1 whole, which is shorter than its diff:
```python
import jax
import jax.numpy as jnp
from jax import lax
from jax.experimental import pallas as pl
from jax.experimental.pallas import tpu as pltpu
from jax.sharding import PartitionSpec as P

MESH = pl.DeviceIdType.MESH
F32 = jnp.float32
BF16 = jnp.bfloat16

SPAN = 192
TOK = 2 * SPAN
GROUP = 4
WIDTH = 128
ROWS = GROUP * SPAN
KROWS = TOK + 16
BIG = 1e30
SCALE = WIDTH**-0.5 * 1.4426950408889634

ORDER = [
    (0, 0),
    (-1, 0), (1, 0), (0, -1), (0, 1),
    (2, 0), (0, 2),
    (-1, -1), (1, 1), (-1, 1), (1, -1),
    (2, -1), (-1, 2), (2, 1), (1, 2),
    (2, 2),
]
SLOT = {place: n for n, place in enumerate(ORDER)}
UNITS = len(ORDER)


def wrap(d):
    return (d + 1) % 4 - 1


def forwards(kind, place):
    first, second = (0, 1) if kind == 0 else (1, 0)
    sends = []

    def send(axis, direction, half):
        there = list(place)
        there[axis] = wrap(there[axis] - direction)
        sends.append((axis, direction, half, SLOT[tuple(there)]))

    if place[second] == 0:
        d = place[first]
        if d == 0:
            send(first, 1, None)
            send(first, -1, None)
        elif d == -1:
            send(first, 1, 0)
        elif d == 1:
            send(first, -1, 1)
        send(second, 1, None)
        send(second, -1, None)
    elif place[second] == -1:
        send(second, 1, 0)
    elif place[second] == 1:
        send(second, -1, 1)
    return sends


def in_halves(kind, place):
    first, second = (0, 1) if kind == 0 else (1, 0)
    return place[second] == 2 or (place[second] == 0 and place[first] == 2)


SENDS = {}
for _kind in range(2):
    for _place in ORDER:
        for _k, _s in enumerate(forwards(_kind, _place)):
            SENDS[(_kind, SLOT[_place], _k)] = len([key for key in SENDS if key[0] == _kind])
N_SENDS = len(SENDS) // 2


def kernel(
    q_ref, k_ref, v_ref, o_ref,
    kbuf, vbuf, qx, qz, oz,
    acc0, acc1, m0, m1, l0, l1, s0, s1, c0, c1,
    send_sem, recv_sem, zsend_sem, zrecv_sem,
):
    accs, maxs, sums = (acc0, acc1), (m0, m1), (l0, l1)
    scores, peaks = (s0, s1), (c0, c1)
    cp = lax.axis_index("cp")
    y, x, z = cp // 8, (cp // 2) % 4, cp % 2
    other = 1 - z

    def device(axis, direction):
        if axis == 0:
            return (y * 4 + (x + direction + 4) % 4) * 2 + z
        return (((y + direction + 4) % 4) * 4 + x) * 2 + z

    partner = (y * 4 + x) * 2 + other

    def part(kind, half):
        if kind == 0:
            return (slice(0, KROWS), slice(0, SPAN), slice(SPAN, KROWS))[0 if half is None else half + 1]
        return (slice(0, WIDTH), slice(0, WIDTH // 2), slice(WIDTH // 2, WIDTH))[0 if half is None else half + 1]

    def view(kind, slot, half):
        buf = kbuf if kind == 0 else vbuf
        return buf.at[slot, part(kind, half)]

    def send_copy(wave, kind, n, k, sends):
        axis, direction, half, there = sends[k]
        if wave == 0 and n == 0:
            src = (k_ref if kind == 0 else v_ref).at[z]
        else:
            src = view(kind, wave * UNITS + n, half)
        return pltpu.make_async_remote_copy(
            src_ref=src,
            dst_ref=view(kind, wave * UNITS + there, half),
            send_sem=send_sem.at[wave, kind, SENDS[(kind, n, k)]],
            recv_sem=recv_sem.at[wave, kind, there, 0 if half is None else half],
            device_id={"cp": device(axis, direction)},
            device_id_type=MESH,
        )

    def forward(wave, n):
        for kind in range(2):
            sends = forwards(kind, ORDER[n])
            for k in range(len(sends)):
                send_copy(wave, kind, n, k, sends).start()

    def arrive(wave, n):
        for kind in range(2):
            for half in (0, 1) if in_halves(kind, ORDER[n]) else (None,):
                here = view(kind, wave * UNITS + n, half)
                pltpu.make_async_remote_copy(
                    src_ref=here,
                    dst_ref=here,
                    send_sem=send_sem.at[wave, kind, 0],
                    recv_sem=recv_sem.at[wave, kind, n, 0 if half is None else half],
                    device_id={"cp": partner},
                    device_id_type=MESH,
                ).wait_recv()
            sends = forwards(kind, ORDER[n])
            for k in range(len(sends)):
                send_copy(wave, kind, n, k, sends).start()

    def z_copy(i):
        src, dst = (
            (k_ref.at[other], kbuf.at[UNITS]),
            (v_ref.at[other], vbuf.at[UNITS]),
            (q_ref.at[other], qz),
            (oz, o_ref.at[z]),
        )[i]
        return pltpu.make_async_remote_copy(
            src_ref=src,
            dst_ref=dst,
            send_sem=zsend_sem.at[i],
            recv_sem=zrecv_sem.at[i],
            device_id={"cp": partner},
            device_id_type=MESH,
        )

    def spread(q, owner, block):
        q = q.astype(F32) * SCALE
        high = q.astype(BF16)
        qx[owner, block, :, 0:WIDTH] = high
        qx[owner, block, :, WIDTH : 2 * WIDTH] = (q - high.astype(F32)).astype(BF16)

    def numbers(slot):
        tile = kbuf[slot, TOK:KROWS, :].astype(F32)
        wide = [jnp.concatenate([tile[8 * h : 8 * h + 1]] * (ROWS // WIDTH), axis=1) for h in range(2)]
        return wide

    def score_stage(owner, pair, block, diagonal=False):
        q = qx[owner, block]
        for a in range(2):
            keys = kbuf[2 * pair + a, 0:TOK, :]
            s = lax.dot_general(
                jnp.concatenate([keys, keys], axis=1), q, (((1,), (1,)), ((), ())), preferred_element_type=F32
            )
            for h in range(2):
                sh = s[h * SPAN : (h + 1) * SPAN]
                if diagonal and a == 0 and h == block:
                    key_off = lax.broadcasted_iota(jnp.int32, (SPAN, SPAN), 0)
                    query_off = lax.broadcasted_iota(jnp.int32, (SPAN, SPAN), 1)
                    seen = jnp.where(key_off <= query_off, 0.0, -BIG).astype(F32)
                    sh = sh + jnp.concatenate([seen] * GROUP, axis=1)
                at = a * TOK + h * SPAN
                scores[block][at : at + SPAN, :] = sh
                top = jnp.max(sh.reshape(SPAN // 8, 8, ROWS), axis=0)
                peaks[block][2 * a + h : 2 * a + h + 1, :] = jnp.max(top, axis=0, keepdims=True)

    def value_stage(owner, pair, block, diagonal=False):
        own = numbers(owner * UNITS)[block]
        old = maxs[block][owner]
        new = old
        seen = []
        for a in range(2):
            for h, number in enumerate(numbers(2 * pair + a)):
                visible = number <= own if diagonal and a == 0 else number < own
                seen.append(visible)
                row = 2 * a + h
                new = jnp.maximum(new, jnp.where(visible, peaks[block][row : row + 1, :], -BIG))
        maxs[block][owner] = new
        fade = jnp.exp2(old - new)
        total = sums[block][owner] * fade
        weights = []
        for i in range(4):
            shift = jnp.where(seen[i], new, BIG)
            p = jnp.exp2(scores[block][i * SPAN : (i + 1) * SPAN, :] - shift)
            total = total + jnp.sum(p.reshape(SPAN // 8, 8, ROWS), axis=0)
            weights.append(p.astype(BF16))
        values = jnp.concatenate([vbuf[2 * pair], vbuf[2 * pair + 1]], axis=1)
        product = jnp.dot(values, jnp.concatenate(weights, axis=0), preferred_element_type=F32)
        accs[block][owner] = accs[block][owner] * fade + product
        sums[block][owner] = total

    def diagonal_step(owner):
        for block in range(2):
            score_stage(owner, owner * (UNITS // 2), block, True)
        for block in range(2):
            value_stage(owner, owner * (UNITS // 2), block, True)

    def finish(owner, block):
        total = jnp.sum(sums[block][owner], axis=0, keepdims=True)
        return (accs[block][owner] / total).T.astype(BF16)

    barrier = pltpu.get_barrier_semaphore()
    neighbours = [device(0, 1), device(0, -1), device(1, 1), device(1, -1), partner]
    for n in neighbours:
        pl.semaphore_signal(barrier, inc=1, device_id={"cp": n}, device_id_type=MESH)
    pl.semaphore_wait(barrier, len(neighbours))

    forward(0, 0)
    for i in range(3):
        z_copy(i).start()
    kbuf[0] = k_ref[z]
    vbuf[0] = v_ref[z]
    for block in range(2):
        spread(q_ref[z, block], 0, block)
        accs[block][...] = jnp.zeros_like(accs[block])
        sums[block][...] = jnp.zeros_like(sums[block])
        maxs[block][...] = jnp.full(maxs[block].shape, -BIG, F32)
    arrive(0, 1)
    diagonal_step(0)
    arrive(0, 2)
    arrive(0, 3)

    half = UNITS // 2
    last = 4 * half - 3

    def place_of(t):
        owner = jnp.where((t >= half - 1) & (t < 3 * half - 2), 1, 0)
        pair = jnp.where(
            t < half - 1,
            t + 1,
            jnp.where(t < 2 * half - 1, t - (half - 1), jnp.where(t < 3 * half - 2, t - (half - 2), t - (2 * half - 2))),
        )
        return owner, pair

    def step(t, carry):
        for k in range(6):

            @pl.when(t == k)
            def _(k=k):
                arrive(0, 2 * k + 4)
                arrive(0, 2 * k + 5)
                if k == 3:
                    z_copy(0).wait_recv()
                    z_copy(1).wait_recv()
                    forward(1, 0)

        @pl.when(t == 6)
        def _():
            arrive(1, 1)
            z_copy(2).wait_recv()
            for block in range(2):
                spread(qz[block], 1, block)
            diagonal_step(1)
            score_stage(0, half - 1, 0)

        for k in range(7):

            @pl.when(t == half - 1 + k)
            def _(k=k):
                arrive(1, 2 * k + 2)
                arrive(1, 2 * k + 3)

        @pl.when(t == 3 * half - 2)
        def _():
            for block in range(2):
                oz[block] = finish(1, block)
            z_copy(3).start()

        owner, pair = place_of(t)
        owner2, pair2 = place_of(jnp.minimum(t + 1, last))
        score_stage(owner, pair, 1)
        value_stage(owner, pair, 0)
        score_stage(owner2, pair2, 0)
        value_stage(owner, pair, 1)
        return carry

    score_stage(0, 1, 0)
    lax.fori_loop(0, last + 1, step, 0)
    for block in range(2):
        o_ref[z, block] = finish(0, block)
    z_copy(3).wait_recv()
    for i in range(4):
        z_copy(i).wait_send()
    for wave in range(2):
        for n in range(UNITS):
            for kind in range(2):
                sends = forwards(kind, ORDER[n])
                for k in range(len(sends)):
                    send_copy(wave, kind, n, k, sends).wait_send()


def attend(q, k, v):
    scratch = [
        pltpu.VMEM((2 * UNITS, KROWS, WIDTH), BF16),
        pltpu.VMEM((2 * UNITS, WIDTH, TOK), BF16),
        pltpu.VMEM((2, 2, ROWS, 2 * WIDTH), BF16),
        pltpu.VMEM((2, ROWS, WIDTH), BF16),
        pltpu.VMEM((2, ROWS, WIDTH), BF16),
    ]
    for shape in [(2, WIDTH, ROWS)] * 2 + [(2, 1, ROWS)] * 2 + [(2, 8, ROWS)] * 2 + [(2 * TOK, ROWS)] * 2 + [(8, ROWS)] * 2:
        scratch.append(pltpu.VMEM(shape, F32))
    scratch += [
        pltpu.SemaphoreType.DMA((2, 2, N_SENDS)),
        pltpu.SemaphoreType.DMA((2, 2, UNITS, 2)),
        pltpu.SemaphoreType.DMA((4,)),
        pltpu.SemaphoreType.DMA((4,)),
    ]
    return pl.pallas_call(
        kernel,
        out_shape=jax.ShapeDtypeStruct((2, 2, ROWS, WIDTH), BF16),
        in_specs=[pl.BlockSpec(memory_space=pltpu.VMEM)] * 3,
        out_specs=pl.BlockSpec(memory_space=pltpu.VMEM),
        scratch_shapes=scratch,
        compiler_params=pltpu.CompilerParams(collective_id=0, has_side_effects=True, vmem_limit_bytes=56 << 20),
    )(q, k, v)


def body(queries, keys, values, positions):
    q = queries.reshape(2, SPAN, 2, GROUP, WIDTH).transpose(2, 0, 3, 1, 4).reshape(2, 2, ROWS, WIDTH)
    numbers = jnp.repeat(jnp.stack([positions[0], positions[SPAN]]) // SPAN, 8).astype(BF16)
    numbers = jnp.broadcast_to(numbers[None, :, None], (2, 16, WIDTH))
    k = jnp.concatenate([keys.transpose(1, 0, 2), numbers], axis=1)
    v = values.transpose(1, 2, 0)
    out = attend(q, k, v).reshape(2, 2, GROUP, SPAN, WIDTH)
    return out.transpose(1, 3, 0, 2, 4).reshape(TOK, 2 * GROUP, WIDTH)


def solution(mesh):
    return jax.shard_map(
        body,
        mesh=mesh,
        in_specs=(P("cp", "tp", None), P("cp", "tp", None), P("cp", "tp", None), P("cp")),
        out_specs=P("cp", "tp", None),
        check_vma=False,
    )
```

time: 308 us -> 105 us (0.34)
  matrix products: 109 us -> 0 us
  waiting for transfers between devices: 100 us -> 0 us
  Pallas kernels: 0 us -> 93.6 us
  other arithmetic: 57.7 us -> 2.17 us
  blocking collectives: 21.3 us -> 0 us
  between operations: 14.1 us -> 0.02 us
    dot_general x2 -> x0, matrix products: 109 us -> none  [the longest x1 54.7 us: attend(): jnp.einsum('grqk,kgd->grqd', expo.astype(jnp.bfloat16), value_rows, prefe...]
    all_gather x1 -> x0, waiting for transfers between devices: 100 us -> none  [body(): piece = lax.all_gather(stacked, 'cp', axis=1, tiled=True)]
    pallas_call x0 -> x1, Pallas kernels: none -> 93.6 us  [attend(): pl.pallas_call(kernel, out_shape=jax.ShapeDtypeStruct((2, 2, ROWS, WIDTH)...]
    reduce_sum x2 -> x0, other arithmetic: 48.1 us -> none  [the longest x1 47.5 us: attend(): total = jnp.sum(expo, axis=-1)]
    unnamed x1 -> x0, blocking collectives: 21.3 us -> none
    ge x1 -> x0, other arithmetic: 7.42 us -> none  [attend(): visible = query_pos[:, None] >= key_pos[None, :]]
  transfers between devices with their start and end apart: 1 -> 0, of which waited for: 1 -> 0; matrix products, arithmetic and copies ran while one was open for 4% -> 0% of each run, Pallas kernels for 0% -> 0%
where the time goes in v1:
time: 105 us; the launch traced here: 104 us
  Pallas kernels  93.6 us (89%)
  local copies, waits for them, and re-layouts  7.9 us (8%)
  other arithmetic  2.17 us (2%)
    pallas_call x1, Pallas kernels, attend(): pl.pallas_call(kernel, out_shape=jax.ShapeDtypeStruct((2, 2, ROWS, WIDTH)...  93.6 us
    unnamed x4, local copies, waits for them, and re-layouts  2.71 us
    transpose x1, local copies, waits for them, and re-layouts, body(): return out.transpose(1, 3, 0, 2, 4).reshape(TOK, 2 * GROUP, WIDTH)  2.62 us

profile of v1, /device:TPU:0, one launch (start us, length us, event | category | flops | bytes accessed | tf_op | source)
XLA Modules:
  0.0 103.7 jit_solution(3184345924887220738)
XLA Ops:
  0.0 0.0 copy-start
  0.0 1.4 %fusion.1 = (s32[1]{0:T(128)}, s32[1]{0:T(128)}) fusion(s32[384]{0:T(512)} %param.7), kind=kLoop, calls=%fused_computation.5 | loop fusion | bytes 16 | tf_op jit(solution)/shard_map/slice | solution.py:341
  1.4 1.4 %fusion = bf16[2]{0:T(256)(128)(2,1)S(1)} fusion(s32[1]{0:T(128)} %get-tuple-element.6, s32[1]{0:T(128)} %get-tuple-element.5), kind=kLoop, calls=%fused_computation.4 | loop fusion | flops 20 | bytes 12 | tf_op jit(solution)/shard_map/convert_element_type | solution.py:341
  2.7 0.1 broadcast_in_dim.4
  2.8 0.1 reshape.23
  2.9 1.0 copy.10
  3.9 0.8 pad_maximum_fusion.k_ref
  4.7 1.8 %copy.7 = bf16[384,2,128]{0,2,1:T(8,128)(2,1)} copy(bf16[384,2,128]{2,1,0:T(2,128)(2,1)} %param.6) | data formatting | bytes 393216 | tf_op args[2]
  6.4 0.0 copy-done
  6.4 1.0 copy.5
  7.5 93.6 %shard_map.46 = bf16[2,2,768,128]{3,2,1,0:T(8,128)(2,1)} custom-call(bf16[2,2,768,128]{3,2,1,0:T(8,128)(2,1)} %bitcast.13, bf16[2,400,128]{2,1,0:T(8,128)(2,1)} %pad_maximum_fusion.k_ref, bf16[2,128,384]{2,1,0:T(8,128)(2,1)} %bitcast.16), custom_call_target="tpu_custom_call" | custom-call | tf_op jit(solution)/shard_map/pallas_call | solution.py:329
  101.1 2.6 %copy.8 = bf16[2,192,2,4,128]{4,3,2,1,0:T(4,128)(2,1)} copy(bf16[2,192,2,4,128]{4,1,3,0,2:T(8,128)(2,1)} %bitcast.12) | data formatting | bytes 1572864 | tf_op jit(solution)/shard_map/transpose | solution.py:346
  (1 shorter events, 0.0 us)
Async XLA Ops:
  0.0 6.4 %copy-start = (bf16[384,8,128]{2,1,0:T(8,128)(2,1)S(1)}, bf16[384,8,128]{2,1,0:T(8,128)(2,1)}, u32[]{:S(2)}) copy-start(bf16[384,8,128]{2,1,0:T(8,128)(2,1)} %param.4) | copy-start | bytes 2359300

commit v2 on v0

v2 whole, which is shorter than its diff:
```python
import jax
import jax.numpy as jnp
from jax import lax
from jax.experimental import pallas as pl
from jax.experimental.pallas import tpu as pltpu
from jax.sharding import PartitionSpec as P

LOGICAL = pl.DeviceIdType.LOGICAL
F32 = jnp.float32
BF16 = jnp.bfloat16

SPAN = 192
TOK = 2 * SPAN
GROUP = 4
WIDTH = 128
ROWS = GROUP * SPAN
KROWS = TOK + 16
UROWS = KROWS + TOK
BIG = 1e30
SCALE = WIDTH**-0.5 * 1.4426950408889634

ORDER = [
    (0, 0),
    (-1, 0), (1, 0), (0, -1), (0, 1),
    (2, 0), (0, 2),
    (-1, -1), (1, 1), (-1, 1), (1, -1),
    (2, -1), (-1, 2), (2, 1), (1, 2),
    (2, 2),
]
UNITS = len(ORDER)
PAIRS = [[(0, 0), (1, 0)]]
for _wave in range(2):
    for _unit in range(1, 15, 2):
        PAIRS.append([(_wave, _unit), (_wave, _unit + 1)])
PAIRS.append([(0, 15), (1, 15)])
SLOT = {unit: 2 * r + a for r, pair in enumerate(PAIRS) for a, unit in enumerate(pair)}

RUNS = [(0, 1, 3), (1, 1, 3), (0, 4, 2), (1, 4, 2), (0, 6, 2), (1, 6, 2), (1, 8, 8), (0, 8, 8)]
STEPS = sum(run[2] for run in RUNS)
SERVICE = {
    1: [(0, 5), (0, 6)],
    4: [(0, 7), (0, 8), (0, 9), (0, 10)],
    7: [(0, 11), (0, 12), (0, 13), (0, 14)],
    9: [(0, 15)],
    10: [(1, 1), (1, 2), (1, 3), (1, 4)],
    12: [(1, 5), (1, 6)],
    15: [(1, 7), (1, 8), (1, 9), (1, 10)],
    18: [(1, 11), (1, 12), (1, 13), (1, 14)],
    20: [(1, 15)],
}
QUERIES_AT = 2
KEYS_AT = 5
DIAGONAL_AT = 6
OUTPUT_AT = 22


def wrap(d):
    return (d + 1) % 4 - 1


def forwards(wave, kind, n):
    place = ORDER[n]
    first, second = (0, 1) if kind == 0 else (1, 0)
    sends = []

    def send(axis, direction):
        there = list(place)
        there[axis] = wrap(there[axis] - direction)
        sends.append((axis, direction, ORDER.index(tuple(there))))

    around = 1 if wave == 0 else -1
    if place[second] == 0:
        if place[first] == 0:
            send(first, 1)
            send(first, -1)
        elif place[first] == -around:
            send(first, around)
        send(second, 1)
        send(second, -1)
    else:
        way = 1 if place[first] in (0, around) else -1
        if place[second] == -way:
            send(second, way)
    return sends


def kernel(
    q_ref, k_ref, v_ref, p_ref, o_ref,
    buf, kvz, qx, qs, qz, oz, qf, kf, vf, ids,
    acc0, acc1, m0, m1, l0, l1, s0, s1, c0, c1,
    send_sem, recv_sem, zsend_sem, zrecv_sem,
):
    accs, maxs, sums = (acc0, acc1), (m0, m1), (l0, l1)
    scores, peaks = (s0, s1), (c0, c1)
    cp = lax.axis_index("cp")
    y, x, z = cp // 8, (cp // 2) % 4, cp % 2
    other = 1 - z

    base = lax.axis_index("tp") * 32 + z
    device = {
        (0, 1): base + (y * 4 + (x + 1) % 4) * 2,
        (0, -1): base + (y * 4 + (x + 3) % 4) * 2,
        (1, 1): base + (((y + 1) % 4) * 4 + x) * 2,
        (1, -1): base + (((y + 3) % 4) * 4 + x) * 2,
    }
    partner = base + (y * 4 + x) * 2 + other - z

    def rows(kind):
        return slice(0, KROWS) if kind == 0 else slice(KROWS, UROWS)

    def copy(src, dst, ssem, rsem, target):
        return pltpu.make_async_remote_copy(
            src_ref=src,
            dst_ref=dst,
            send_sem=ssem,
            recv_sem=rsem,
            device_id=target,
            device_id_type=LOGICAL,
        )

    def forward(wave, n):
        for kind in range(2):
            for axis, direction, there in forwards(wave, kind, n):
                copy(
                    buf.at[SLOT[(wave, n)], rows(kind)],
                    buf.at[SLOT[(wave, there)], rows(kind)],
                    send_sem.at[wave],
                    recv_sem.at[wave, there],
                    device[axis, direction],
                ).start()

    def arrive(wave, n):
        here = buf.at[SLOT[(wave, n)]]
        copy(here, here, send_sem.at[wave], recv_sem.at[wave, n], partner).wait_recv()
        forward(wave, n)

    def z_copy(i):
        src, dst = (
            (qs, qz),
            (kvz, buf.at[SLOT[(1, 0)]]),
            (oz, o_ref.at[z]),
        )[i]
        return copy(src, dst, zsend_sem.at[i], zrecv_sem.at[i], partner)

    def spread(q, owner, block, h):
        q = q * SCALE
        high = q.astype(BF16)
        rows = slice(h * SPAN, (h + 1) * SPAN)
        qx[owner, block, rows, 0:WIDTH] = high
        qx[owner, block, rows, WIDTH : 2 * WIDTH] = (q - high.astype(F32)).astype(BF16)

    def head(owner_z, block, h):
        return qf[pl.ds(block * SPAN * 2 * GROUP + GROUP * owner_z + h, SPAN, stride=2 * GROUP), :]

    def spread_keys():
        kf[...] = k_ref[...].astype(F32)
        vf[...] = v_ref[...].astype(F32)
        blocks = [jnp.full((8, WIDTH), p_ref[b * SPAN] // SPAN, jnp.int32).astype(F32) for b in range(2)]
        for b in range(2):
            ids[0, b] = blocks[b]
            qs[b, ROWS:, :] = jnp.concatenate([blocks[b]] * 2, axis=0).astype(BF16)
        for served, put in ((z, buf.at[0]), (other, kvz)):
            put[0:TOK, :] = kf[pl.ds(served, TOK, stride=2), :].astype(BF16)
            put[TOK:KROWS, :] = jnp.concatenate(blocks, axis=0).astype(BF16)
            for c in range(TOK // WIDTH):
                v = vf[pl.ds(2 * WIDTH * c + served, WIDTH, stride=2), :]
                put[KROWS + c * WIDTH : KROWS + (c + 1) * WIDTH, :] = v.T.astype(BF16)

    def wide(tile):
        return jnp.concatenate([tile[0:1]] * (ROWS // WIDTH), axis=1)

    def numbers(slot):
        tile = buf[slot, TOK:KROWS, :].astype(F32)
        return [wide(tile[8 * h : 8 * h + 8]) for h in range(2)]

    def score_stage(owner, slots, block, diagonal=None):
        q = qx[owner, block]
        for a, slot in enumerate(slots):
            keys = buf[slot, 0:TOK, :]
            s = lax.dot_general(
                jnp.concatenate([keys, keys], axis=1), q, (((1,), (1,)), ((), ())), preferred_element_type=F32
            )
            for h in range(2):
                sh = s[h * SPAN : (h + 1) * SPAN]
                if diagonal == a and h == block:
                    key_off = lax.broadcasted_iota(jnp.int32, (SPAN, SPAN), 0)
                    query_off = lax.broadcasted_iota(jnp.int32, (SPAN, SPAN), 1)
                    seen = jnp.where(key_off <= query_off, 0.0, -BIG).astype(F32)
                    sh = sh + jnp.concatenate([seen] * GROUP, axis=1)
                at = a * TOK + h * SPAN
                scores[block][at : at + SPAN, :] = sh
                top = jnp.max(sh.reshape(SPAN // 8, 8, ROWS), axis=0)
                peaks[block][2 * a + h : 2 * a + h + 1, :] = jnp.max(top, axis=0, keepdims=True)

    def value_stage(owner, slots, block, diagonal=None):
        own = wide(ids[owner, block])
        old = maxs[block][owner]
        new = old
        seen = []
        for a, slot in enumerate(slots):
            for h, number in enumerate(numbers(slot)):
                visible = number <= own if diagonal == a else number < own
                seen.append(visible)
                row = 2 * a + h
                new = jnp.maximum(new, jnp.where(visible, peaks[block][row : row + 1, :], -BIG))
        maxs[block][owner] = new
        fade = jnp.exp2(old - new)
        total = sums[block][owner] * fade
        weights = []
        for i, visible in enumerate(seen):
            shift = jnp.where(visible, new, BIG)
            p = jnp.exp2(scores[block][i * SPAN : (i + 1) * SPAN, :] - shift)
            total = total + jnp.sum(p.reshape(SPAN // 8, 8, ROWS), axis=0)
            weights.append(p.astype(BF16))
        values = jnp.concatenate(
            [buf[slot, KROWS + c * WIDTH : KROWS + (c + 1) * WIDTH, :] for slot in slots for c in range(TOK // WIDTH)],
            axis=1,
        )
        product = jnp.dot(values, jnp.concatenate(weights, axis=0), preferred_element_type=F32)
        accs[block][owner] = accs[block][owner] * fade + product
        sums[block][owner] = total

    def single_step(owner, slots, diagonal):
        for block in range(2):
            score_stage(owner, slots, block, diagonal)
        for block in range(2):
            value_stage(owner, slots, block, diagonal)

    def finish(owner, block):
        total = jnp.sum(sums[block][owner], axis=0, keepdims=True)
        return (accs[block][owner] / total).T.astype(BF16)

    barrier = pltpu.get_barrier_semaphore()
    neighbours = [*device.values(), partner]
    for n in neighbours:
        pl.semaphore_signal(barrier, inc=1, device_id=n, device_id_type=LOGICAL)
    spread_keys()
    pl.semaphore_wait(barrier, len(neighbours))

    forward(0, 0)
    qf[...] = q_ref[...].astype(F32)
    for block in range(2):
        for h in range(GROUP):
            qs[block, h * SPAN : (h + 1) * SPAN, :] = head(other, block, h).astype(BF16)
    z_copy(0).start()
    z_copy(1).start()
    for block in range(2):
        for h in range(GROUP):
            spread(head(z, block, h), 0, block, h)
        accs[block][...] = jnp.zeros_like(accs[block])
        sums[block][...] = jnp.zeros_like(sums[block])
        maxs[block][...] = jnp.full(maxs[block].shape, -BIG, F32)
    single_step(0, [0], 0)
    for n in range(1, 5):
        arrive(0, n)

    def place_of(t):
        owner, pair, begin = jnp.int32(0), t, 0
        for own, first, pairs in RUNS:
            owner = jnp.where(t >= begin, own, owner)
            pair = jnp.where(t >= begin, t - begin + first, pair)
            begin += pairs
        return owner, [2 * pair, 2 * pair + 1]

    def queries_come():
        z_copy(0).wait_recv()
        for block in range(2):
            ids[1, block] = qz[block, ROWS:, :].astype(F32)[0:8]
            for h in range(GROUP):
                spread(qz[block, h * SPAN : (h + 1) * SPAN, :].astype(F32), 1, block, h)

    def keys_come():
        z_copy(1).wait_recv()
        forward(1, 0)

    def diagonal_meets():
        single_step(0, [1], None)
        single_step(1, [0, 1], 1)
        owner, slots = place_of(jnp.int32(DIAGONAL_AT))
        score_stage(owner, slots, 0)

    def outputs_go():
        for block in range(2):
            oz[block] = finish(1, block)
        z_copy(2).start()

    events = {at: [lambda unit=unit: arrive(*unit) for unit in units] for at, units in SERVICE.items()}
    for at, event in (
        (QUERIES_AT, queries_come),
        (KEYS_AT, keys_come),
        (DIAGONAL_AT, diagonal_meets),
        (OUTPUT_AT, outputs_go),
    ):
        events.setdefault(at, []).append(event)
    starts = sorted(events)

    def step(t, carry):
        owner, slots = place_of(t)
        owner2, slots2 = place_of(jnp.minimum(t + 1, STEPS - 1))
        score_stage(owner, slots, 1)
        value_stage(owner, slots, 0)
        score_stage(owner2, slots2, 0)
        value_stage(owner, slots, 1)
        return carry

    def stretch(e, carry):
        begin, end = jnp.int32(0), jnp.int32(STEPS)
        for i, at in enumerate(starts):
            begin = jnp.where(e == i + 1, at, begin)
            end = jnp.where(e == i, at, end)

            @pl.when(e == i + 1)
            def _(at=at):
                for event in events[at]:
                    event()

        return lax.fori_loop(begin, end, step, carry)

    score_stage(0, [2, 3], 0)
    lax.fori_loop(0, len(starts) + 1, stretch, 0)
    for block in range(2):
        o_ref[z, block] = finish(0, block)
    z_copy(2).wait_recv()
    for i in range(3):
        z_copy(i).wait_send()
    for wave in range(2):
        sent = buf.at[0 : UNITS - 1]
        copy(sent, sent, send_sem.at[wave], recv_sem.at[wave, 0], partner).wait_send()


def attend(q, k, v, positions):
    scratch = [
        pltpu.VMEM((2 * UNITS, UROWS, WIDTH), BF16),
        pltpu.VMEM((UROWS, WIDTH), BF16),
        pltpu.VMEM((2, 2, ROWS, 2 * WIDTH), BF16),
        pltpu.VMEM((2, ROWS + 16, WIDTH), BF16),
        pltpu.VMEM((2, ROWS + 16, WIDTH), BF16),
        pltpu.VMEM((2, ROWS, WIDTH), BF16),
        pltpu.VMEM(q.shape, F32),
        pltpu.VMEM(k.shape, F32),
        pltpu.VMEM(v.shape, F32),
        pltpu.VMEM((2, 2, 8, WIDTH), F32),
    ]
    for shape in [(2, WIDTH, ROWS)] * 2 + [(2, 1, ROWS)] * 2 + [(2, 8, ROWS)] * 2 + [(2 * TOK, ROWS)] * 2 + [(8, ROWS)] * 2:
        scratch.append(pltpu.VMEM(shape, F32))
    scratch += [
        pltpu.SemaphoreType.DMA((2,)),
        pltpu.SemaphoreType.DMA((2, UNITS)),
        pltpu.SemaphoreType.DMA((3,)),
        pltpu.SemaphoreType.DMA((3,)),
    ]
    return pl.pallas_call(
        kernel,
        out_shape=jax.ShapeDtypeStruct((2, 2, ROWS, WIDTH), BF16),
        in_specs=[pl.BlockSpec(memory_space=pltpu.VMEM)] * 3 + [pl.BlockSpec(memory_space=pltpu.SMEM)],
        out_specs=pl.BlockSpec(memory_space=pltpu.VMEM),
        scratch_shapes=scratch,
        compiler_params=pltpu.CompilerParams(collective_id=0, has_side_effects=True, vmem_limit_bytes=56 << 20),
    )(q, k, v, positions)


def body(queries, keys, values, positions):
    rows = [a.reshape(-1, WIDTH) for a in (queries, keys, values)]
    out = attend(*rows, positions).reshape(2, 2, GROUP, SPAN, WIDTH)
    return out.transpose(1, 3, 0, 2, 4).reshape(TOK, 2 * GROUP, WIDTH)


def solution(mesh):
    return jax.shard_map(
        body,
        mesh=mesh,
        in_specs=(P("cp", "tp", None), P("cp", "tp", None), P("cp", "tp", None), P("cp")),
        out_specs=P("cp", "tp", None),
        check_vma=False,
    )
```

time: 308 us -> 80.8 us (0.26)
  matrix products: 109 us -> 0 us
  waiting for transfers between devices: 100 us -> 0 us
  Pallas kernels: 0 us -> 78 us
  other arithmetic: 57.7 us -> 0 us
  blocking collectives: 21.3 us -> 0 us
  between operations: 14.1 us -> 0.01 us
    dot_general x2 -> x0, matrix products: 109 us -> none  [the longest x1 54.7 us: attend(): jnp.einsum('grqk,kgd->grqd', expo.astype(jnp.bfloat16), value_rows, prefe...]
    all_gather x1 -> x0, waiting for transfers between devices: 100 us -> none  [body(): piece = lax.all_gather(stacked, 'cp', axis=1, tiled=True)]
    pallas_call x0 -> x1, Pallas kernels: none -> 78 us  [attend(): pl.pallas_call(kernel, out_shape=jax.ShapeDtypeStruct((2, 2, ROWS, WIDTH)...]
    reduce_sum x2 -> x0, other arithmetic: 48.1 us -> none  [the longest x1 47.5 us: attend(): total = jnp.sum(expo, axis=-1)]
    unnamed x1 -> x0, blocking collectives: 21.3 us -> none
    ge x1 -> x0, other arithmetic: 7.42 us -> none  [attend(): visible = query_pos[:, None] >= key_pos[None, :]]
  transfers between devices with their start and end apart: 1 -> 0, of which waited for: 1 -> 0; matrix products, arithmetic and copies ran while one was open for 4% -> 0% of each run, Pallas kernels for 0% -> 0%
where the time goes in v2:
time: 80.8 us; the launch traced here: 80.7 us
  Pallas kernels  78 us (97%)
  local copies, waits for them, and re-layouts  2.62 us (3%)
    pallas_call x1, Pallas kernels, attend(): pl.pallas_call(kernel, out_shape=jax.ShapeDtypeStruct((2, 2, ROWS, WIDTH)...  78 us
    transpose x1, local copies, waits for them, and re-layouts, body(): return out.transpose(1, 3, 0, 2, 4).reshape(TOK, 2 * GROUP, WIDTH)  2.62 us

profile of v2, /device:TPU:0, one launch (start us, length us, event | category | flops | bytes accessed | tf_op | source)
XLA Modules:
  0.0 80.7 jit_solution(9213843478495779871)
XLA Ops:
  0.0 78.0 %shard_map.46 = bf16[2,2,768,128]{3,2,1,0:T(8,128)(2,1)} custom-call(bf16[3072,128]{1,0:T(8,128)(2,1)} %bitcast.8, bf16[768,128]{1,0:T(8,128)(2,1)} %bitcast.9, bf16[768,128]{1,0:T(8,128)(2,1)} %bitcast.10, s32[384]{0:T(512)} %p_ref.1), custom_call_target="tpu_custom_call" | custom-call | tf_op jit(solution)/shard_map/pallas_call | solution.py:352
  78.0 2.6 %copy.5 = bf16[2,192,2,4,128]{4,3,2,1,0:T(4,128)(2,1)} copy(bf16[2,192,2,4,128]{4,1,3,0,2:T(8,128)(2,1)} %bitcast.7) | data formatting | bytes 1572864 | tf_op jit(solution)/shard_map/transpose | solution.py:365

commit v3 on v2

--- a/solution.py
+++ b/solution.py
@@ -35,23 +35,26 @@
 PAIRS.append([(0, 15), (1, 15)])
 SLOT = {unit: 2 * r + a for r, pair in enumerate(PAIRS) for a, unit in enumerate(pair)}
 
-RUNS = [(0, 1, 3), (1, 1, 3), (0, 4, 2), (1, 4, 2), (0, 6, 2), (1, 6, 2), (1, 8, 8), (0, 8, 8)]
+RUNS = [
+    (0, 1, 2), (1, 1, 2), (0, 3, 1), (1, 3, 1), (0, 4, 2), (1, 4, 2), (0, 6, 2), (1, 6, 2),
+    (1, 8, 4), (0, 8, 1), (1, 12, 4), (0, 9, 7),
+]
 STEPS = sum(run[2] for run in RUNS)
 SERVICE = {
-    1: [(0, 5), (0, 6)],
+    3: [(0, 5), (0, 6)],
     4: [(0, 7), (0, 8), (0, 9), (0, 10)],
-    7: [(0, 11), (0, 12), (0, 13), (0, 14)],
-    9: [(0, 15)],
-    10: [(1, 1), (1, 2), (1, 3), (1, 4)],
+    8: [(1, 1), (1, 2), (1, 3), (1, 4)],
+    9: [(0, 11), (0, 12), (0, 13), (0, 14)],
+    11: [(0, 15)],
     12: [(1, 5), (1, 6)],
-    15: [(1, 7), (1, 8), (1, 9), (1, 10)],
+    14: [(1, 7), (1, 8), (1, 9), (1, 10)],
     18: [(1, 11), (1, 12), (1, 13), (1, 14)],
     20: [(1, 15)],
 }
-QUERIES_AT = 2
-KEYS_AT = 5
+QUERIES_AT = 1
+KEYS_AT = 4
 DIAGONAL_AT = 6
-OUTPUT_AT = 22
+OUTPUT_AT = 23
 
 
 def wrap(d):
@@ -78,7 +81,7 @@
         send(second, 1)
         send(second, -1)
     else:
-        way = 1 if place[first] in (0, around) else -1
+        way = -1 if place[first] in (0, around) else 1
         if place[second] == -way:
             send(second, way)
     return sends
@@ -118,21 +121,22 @@
             device_id_type=LOGICAL,
         )
 
-    def forward(wave, n):
-        for kind in range(2):
-            for axis, direction, there in forwards(wave, kind, n):
-                copy(
-                    buf.at[SLOT[(wave, n)], rows(kind)],
-                    buf.at[SLOT[(wave, there)], rows(kind)],
-                    send_sem.at[wave],
-                    recv_sem.at[wave, there],
-                    device[axis, direction],
-                ).start()
-
-    def arrive(wave, n):
-        here = buf.at[SLOT[(wave, n)]]
-        copy(here, here, send_sem.at[wave], recv_sem.at[wave, n], partner).wait_recv()
-        forward(wave, n)
+    def forward(units):
+        sends = [(*send, kind, wave, n) for wave, n in units for kind in range(2) for send in forwards(wave, kind, n)]
+        for axis, direction, there, kind, wave, n in sorted(sends, key=lambda send: send[2]):
+            copy(
+                buf.at[SLOT[(wave, n)], rows(kind)],
+                buf.at[SLOT[(wave, there)], rows(kind)],
+                send_sem.at[wave],
+                recv_sem.at[wave, there],
+                device[axis, direction],
+            ).start()
+
+    def arrive(units):
+        for wave, n in units:
+            here = buf.at[SLOT[(wave, n)]]
+            copy(here, here, send_sem.at[wave], recv_sem.at[wave, n], partner).wait_recv()
+        forward(units)
 
     def z_copy(i):
         src, dst = (
@@ -237,7 +241,7 @@
     spread_keys()
     pl.semaphore_wait(barrier, len(neighbours))
 
-    forward(0, 0)
+    forward([(0, 0)])
     qf[...] = q_ref[...].astype(F32)
     for block in range(2):
         for h in range(GROUP):
@@ -251,8 +255,7 @@
         sums[block][...] = jnp.zeros_like(sums[block])
         maxs[block][...] = jnp.full(maxs[block].shape, -BIG, F32)
     single_step(0, [0], 0)
-    for n in range(1, 5):
-        arrive(0, n)
+    arrive([(0, n) for n in range(1, 5)])
 
     def place_of(t):
         owner, pair, begin = jnp.int32(0), t, 0
@@ -271,7 +274,7 @@
 
     def keys_come():
         z_copy(1).wait_recv()
-        forward(1, 0)
+        forward([(1, 0)])
 
     def diagonal_meets():
         single_step(0, [1], None)
@@ -284,14 +287,14 @@
             oz[block] = finish(1, block)
         z_copy(2).start()
 
-    events = {at: [lambda unit=unit: arrive(*unit) for unit in units] for at, units in SERVICE.items()}
+    events = {at: [lambda units=units: arrive(units)] for at, units in SERVICE.items()}
     for at, event in (
         (QUERIES_AT, queries_come),
         (KEYS_AT, keys_come),
         (DIAGONAL_AT, diagonal_meets),
         (OUTPUT_AT, outputs_go),
     ):
-        events.setdefault(at, []).append(event)
+        events.setdefault(at, []).insert(0, event)
     starts = sorted(events)
 
     def step(t, carry):

time: 80.8 us -> 72.6 us (0.90)
  Pallas kernels: 78 us -> 69.8 us
    pallas_call x1, Pallas kernels: 78 us -> 69.8 us  [attend(): pl.pallas_call(kernel, out_shape=jax.ShapeDtypeStruct((2, 2, ROWS, WIDTH)...]
where the time goes in v3:
time: 72.6 us; the launch traced here: 72.5 us
  Pallas kernels  69.8 us (96%)
  local copies, waits for them, and re-layouts  2.62 us (4%)
    pallas_call x1, Pallas kernels, attend(): pl.pallas_call(kernel, out_shape=jax.ShapeDtypeStruct((2, 2, ROWS, WIDTH)...  69.8 us
    transpose x1, local copies, waits for them, and re-layouts, body(): return out.transpose(1, 3, 0, 2, 4).reshape(TOK, 2 * GROUP, WIDTH)  2.62 us

profile of v3, /device:TPU:0, one launch (start us, length us, event | category | flops | bytes accessed | tf_op | source)
XLA Modules:
  0.0 72.5 jit_solution(14188199850663437796)
XLA Ops:
  0.0 69.8 %shard_map.46 = bf16[2,2,768,128]{3,2,1,0:T(8,128)(2,1)} custom-call(bf16[3072,128]{1,0:T(8,128)(2,1)} %bitcast.8, bf16[768,128]{1,0:T(8,128)(2,1)} %bitcast.9, bf16[768,128]{1,0:T(8,128)(2,1)} %bitcast.10, s32[384]{0:T(512)} %p_ref.1), custom_call_target="tpu_custom_call" | custom-call | tf_op jit(solution)/shard_map/pallas_call | solution.py:355
  69.8 2.6 %copy.5 = bf16[2,192,2,4,128]{4,3,2,1,0:T(4,128)(2,1)} copy(bf16[2,192,2,4,128]{4,1,3,0,2:T(8,128)(2,1)} %bitcast.7) | data formatting | bytes 1572864 | tf_op jit(solution)/shard_map/transpose | solution.py:368

commit v4 on v3

--- a/solution.py
+++ b/solution.py
@@ -43,12 +43,11 @@
 SERVICE = {
     3: [(0, 5), (0, 6)],
     4: [(0, 7), (0, 8), (0, 9), (0, 10)],
-    8: [(1, 1), (1, 2), (1, 3), (1, 4)],
-    9: [(0, 11), (0, 12), (0, 13), (0, 14)],
-    11: [(0, 15)],
-    12: [(1, 5), (1, 6)],
-    14: [(1, 7), (1, 8), (1, 9), (1, 10)],
-    18: [(1, 11), (1, 12), (1, 13), (1, 14)],
+    7: [(1, 1), (1, 2), (1, 3), (1, 4)],
+    8: [(0, 11), (0, 12), (0, 13), (0, 14)],
+    11: [(0, 15), (1, 5), (1, 6)],
+    13: [(1, 7), (1, 8), (1, 9), (1, 10)],
+    17: [(1, 11), (1, 12), (1, 13), (1, 14)],
     20: [(1, 15)],
 }
 QUERIES_AT = 1
@@ -140,7 +139,8 @@
 
     def z_copy(i):
         src, dst = (
-            (qs, qz),
+            (qs.at[0], qz.at[0]),
+            (qs.at[1], qz.at[1]),
             (kvz, buf.at[SLOT[(1, 0)]]),
             (oz, o_ref.at[z]),
         )[i]
@@ -246,8 +246,8 @@
     for block in range(2):
         for h in range(GROUP):
             qs[block, h * SPAN : (h + 1) * SPAN, :] = head(other, block, h).astype(BF16)
-    z_copy(0).start()
-    z_copy(1).start()
+        z_copy(block).start()
+    z_copy(2).start()
     for block in range(2):
         for h in range(GROUP):
             spread(head(z, block, h), 0, block, h)
@@ -265,15 +265,14 @@
             begin += pairs
         return owner, [2 * pair, 2 * pair + 1]
 
-    def queries_come():
-        z_copy(0).wait_recv()
-        for block in range(2):
-            ids[1, block] = qz[block, ROWS:, :].astype(F32)[0:8]
-            for h in range(GROUP):
-                spread(qz[block, h * SPAN : (h + 1) * SPAN, :].astype(F32), 1, block, h)
+    def queries_come(block):
+        z_copy(block).wait_recv()
+        ids[1, block] = qz[block, ROWS:, :].astype(F32)[0:8]
+        for h in range(GROUP):
+            spread(qz[block, h * SPAN : (h + 1) * SPAN, :].astype(F32), 1, block, h)
 
     def keys_come():
-        z_copy(1).wait_recv()
+        z_copy(2).wait_recv()
         forward([(1, 0)])
 
     def diagonal_meets():
@@ -285,11 +284,12 @@
     def outputs_go():
         for block in range(2):
             oz[block] = finish(1, block)
-        z_copy(2).start()
+        z_copy(3).start()
 
     events = {at: [lambda units=units: arrive(units)] for at, units in SERVICE.items()}
     for at, event in (
-        (QUERIES_AT, queries_come),
+        (QUERIES_AT, lambda: queries_come(0)),
+        (QUERIES_AT + 1, lambda: queries_come(1)),
         (KEYS_AT, keys_come),
         (DIAGONAL_AT, diagonal_meets),
         (OUTPUT_AT, outputs_go),
@@ -323,8 +323,8 @@
     lax.fori_loop(0, len(starts) + 1, stretch, 0)
     for block in range(2):
         o_ref[z, block] = finish(0, block)
-    z_copy(2).wait_recv()
-    for i in range(3):
+    z_copy(3).wait_recv()
+    for i in range(4):
         z_copy(i).wait_send()
     for wave in range(2):
         sent = buf.at[0 : UNITS - 1]
@@ -349,8 +349,8 @@
     scratch += [
         pltpu.SemaphoreType.DMA((2,)),
         pltpu.SemaphoreType.DMA((2, UNITS)),
-        pltpu.SemaphoreType.DMA((3,)),
-        pltpu.SemaphoreType.DMA((3,)),
+        pltpu.SemaphoreType.DMA((4,)),
+        pltpu.SemaphoreType.DMA((4,)),
     ]
     return pl.pallas_call(
         kernel,

time: 72.6 us -> 70.4 us (0.970)
  Pallas kernels: 69.8 us -> 67.6 us
    pallas_call x1, Pallas kernels: 69.8 us -> 67.6 us  [attend(): pl.pallas_call(kernel, out_shape=jax.ShapeDtypeStruct((2, 2, ROWS, WIDTH)...]
where the time goes in v4:
time: 70.4 us; the launch traced here: 70.2 us
  Pallas kernels  67.6 us (96%)
  local copies, waits for them, and re-layouts  2.62 us (4%)
    pallas_call x1, Pallas kernels, attend(): pl.pallas_call(kernel, out_shape=jax.ShapeDtypeStruct((2, 2, ROWS, WIDTH)...  67.6 us
    transpose x1, local copies, waits for them, and re-layouts, body(): return out.transpose(1, 3, 0, 2, 4).reshape(TOK, 2 * GROUP, WIDTH)  2.62 us

profile of v4, /device:TPU:0, one launch (start us, length us, event | category | flops | bytes accessed | tf_op | source)
XLA Modules:
  0.0 70.2 jit_solution(15433239502796867901)
XLA Ops:
  0.0 67.6 %shard_map.46 = bf16[2,2,768,128]{3,2,1,0:T(8,128)(2,1)} custom-call(bf16[3072,128]{1,0:T(8,128)(2,1)} %bitcast.8, bf16[768,128]{1,0:T(8,128)(2,1)} %bitcast.9, bf16[768,128]{1,0:T(8,128)(2,1)} %bitcast.10, s32[384]{0:T(512)} %p_ref.1), custom_call_target="tpu_custom_call" | custom-call | tf_op jit(solution)/shard_map/pallas_call | solution.py:355
  67.6 2.6 %copy.5 = bf16[2,192,2,4,128]{4,3,2,1,0:T(4,128)(2,1)} copy(bf16[2,192,2,4,128]{4,1,3,0,2:T(8,128)(2,1)} %bitcast.7) | data formatting | bytes 1572864 | tf_op jit(solution)/shard_map/transpose | solution.py:368

commit v5 on v4

--- a/solution.py
+++ b/solution.py
@@ -16,7 +16,7 @@
 ROWS = GROUP * SPAN
 KROWS = TOK + 16
 UROWS = KROWS + TOK
-BIG = 1e30
+BIG = 3.4028235e38
 SCALE = WIDTH**-0.5 * 1.4426950408889634
 
 ORDER = [

time: 70.4 us -> 70.4 us (level)
  no operation moved by 1% of the time
where the time goes in v5:
time: 70.4 us; the launch traced here: 70.2 us
  Pallas kernels  67.6 us (96%)
  local copies, waits for them, and re-layouts  2.62 us (4%)
    pallas_call x1, Pallas kernels, attend(): pl.pallas_call(kernel, out_shape=jax.ShapeDtypeStruct((2, 2, ROWS, WIDTH)...  67.6 us
    transpose x1, local copies, waits for them, and re-layouts, body(): return out.transpose(1, 3, 0, 2, 4).reshape(TOK, 2 * GROUP, WIDTH)  2.62 us

profile of v5, /device:TPU:0, one launch (start us, length us, event | category | flops | bytes accessed | tf_op | source)
XLA Modules:
  0.0 70.2 jit_solution(13981707271014950144)
XLA Ops:
  0.0 67.6 %shard_map.46 = bf16[2,2,768,128]{3,2,1,0:T(8,128)(2,1)} custom-call(bf16[3072,128]{1,0:T(8,128)(2,1)} %bitcast.8, bf16[768,128]{1,0:T(8,128)(2,1)} %bitcast.9, bf16[768,128]{1,0:T(8,128)(2,1)} %bitcast.10, s32[384]{0:T(512)} %p_ref.1), custom_call_target="tpu_custom_call" | custom-call | tf_op jit(solution)/shard_map/pallas_call | solution.py:355
  67.6 2.6 %copy.5 = bf16[2,192,2,4,128]{4,3,2,1,0:T(4,128)(2,1)} copy(bf16[2,192,2,4,128]{4,1,3,0,2:T(8,128)(2,1)} %bitcast.7) | data formatting | bytes 1572864 | tf_op jit(solution)/shard_map/transpose | solution.py:368

commit v6 on v5

--- a/solution.py
+++ b/solution.py
@@ -156,19 +156,16 @@
     def head(owner_z, block, h):
         return qf[pl.ds(block * SPAN * 2 * GROUP + GROUP * owner_z + h, SPAN, stride=2 * GROUP), :]
 
-    def spread_keys():
-        kf[...] = k_ref[...].astype(F32)
-        vf[...] = v_ref[...].astype(F32)
+    def spread_keys(served, put):
         blocks = [jnp.full((8, WIDTH), p_ref[b * SPAN] // SPAN, jnp.int32).astype(F32) for b in range(2)]
-        for b in range(2):
+        for b in range(2) if served is z else ():
             ids[0, b] = blocks[b]
             qs[b, ROWS:, :] = jnp.concatenate([blocks[b]] * 2, axis=0).astype(BF16)
-        for served, put in ((z, buf.at[0]), (other, kvz)):
-            put[0:TOK, :] = kf[pl.ds(served, TOK, stride=2), :].astype(BF16)
-            put[TOK:KROWS, :] = jnp.concatenate(blocks, axis=0).astype(BF16)
-            for c in range(TOK // WIDTH):
-                v = vf[pl.ds(2 * WIDTH * c + served, WIDTH, stride=2), :]
-                put[KROWS + c * WIDTH : KROWS + (c + 1) * WIDTH, :] = v.T.astype(BF16)
+        put[0:TOK, :] = kf[pl.ds(served, TOK, stride=2), :].astype(BF16)
+        put[TOK:KROWS, :] = jnp.concatenate(blocks, axis=0).astype(BF16)
+        for c in range(TOK // WIDTH):
+            v = vf[pl.ds(2 * WIDTH * c + served, WIDTH, stride=2), :]
+            put[KROWS + c * WIDTH : KROWS + (c + 1) * WIDTH, :] = v.T.astype(BF16)
 
     def wide(tile):
         return jnp.concatenate([tile[0:1]] * (ROWS // WIDTH), axis=1)
@@ -238,7 +235,9 @@
     neighbours = [*device.values(), partner]
     for n in neighbours:
         pl.semaphore_signal(barrier, inc=1, device_id=n, device_id_type=LOGICAL)
-    spread_keys()
+    kf[...] = k_ref[...].astype(F32)
+    vf[...] = v_ref[...].astype(F32)
+    spread_keys(z, buf.at[0])
     pl.semaphore_wait(barrier, len(neighbours))
 
     forward([(0, 0)])
@@ -247,6 +246,7 @@
         for h in range(GROUP):
             qs[block, h * SPAN : (h + 1) * SPAN, :] = head(other, block, h).astype(BF16)
         z_copy(block).start()
+    spread_keys(other, kvz)
     z_copy(2).start()
     for block in range(2):
         for h in range(GROUP):

time: 70.4 us -> 70.4 us (level)
  no operation moved by 1% of the time
where the time goes in v6:
time: 70.4 us; the launch traced here: 70.2 us
  Pallas kernels  67.6 us (96%)
  local copies, waits for them, and re-layouts  2.62 us (4%)
    pallas_call x1, Pallas kernels, attend(): pl.pallas_call(kernel, out_shape=jax.ShapeDtypeStruct((2, 2, ROWS, WIDTH)...  67.6 us
    transpose x1, local copies, waits for them, and re-layouts, body(): return out.transpose(1, 3, 0, 2, 4).reshape(TOK, 2 * GROUP, WIDTH)  2.62 us

profile of v6, /device:TPU:0, one launch (start us, length us, event | category | flops | bytes accessed | tf_op | source)
XLA Modules:
  0.0 70.2 jit_solution(14772069076774009447)
XLA Ops:
  0.0 67.6 %shard_map.46 = bf16[2,2,768,128]{3,2,1,0:T(8,128)(2,1)} custom-call(bf16[3072,128]{1,0:T(8,128)(2,1)} %bitcast.8, bf16[768,128]{1,0:T(8,128)(2,1)} %bitcast.9, bf16[768,128]{1,0:T(8,128)(2,1)} %bitcast.10, s32[384]{0:T(512)} %p_ref.1), custom_call_target="tpu_custom_call" | custom-call | tf_op jit(solution)/shard_map/pallas_call | solution.py:355
  67.6 2.6 %copy.5 = bf16[2,192,2,4,128]{4,3,2,1,0:T(4,128)(2,1)} copy(bf16[2,192,2,4,128]{4,1,3,0,2:T(8,128)(2,1)} %bitcast.7) | data formatting | bytes 1572864 | tf_op jit(solution)/shard_map/transpose | solution.py:368
